TPU v7x, 256 devices: a whole 4x4x8 slice. The times are simulated.
256 devices in a mesh: blk: 32 (over z, x_lo, core), quarter: 8 (over y, x_hi).
Axes of the slice: x: 4 (x_hi: 2, x_lo: 2; x = x_hi * 2 + x_lo), y: 4, z: 8, core: 2. Of those that a mesh axis runs over, the one named last changes fastest.
Arguments:
- sensor: bfloat16 [8192, 1024], P(('blk', 'quarter')), may hold values from -24 to 24
- video: bfloat16 [8192, 1024], P(('blk', 'quarter')), may hold values from -24 to 24
- sens_ref: bfloat16 [1024, 1024], replicated, may hold values from -0.25 to 0.25
- vid_ref: bfloat16 [1024, 1024], replicated, may hold values from -0.25 to 0.25
- sens_val: bfloat16 [1024, 1024], replicated, may hold values from -0.1875 to 0.1875
- vid_val: bfloat16 [1024, 1024], replicated, may hold values from -0.1875 to 0.1875
- sens_out: bfloat16 [1024, 1024], replicated, may hold values from -0.1875 to 0.1875
- vid_out: bfloat16 [1024, 1024], replicated, may hold values from -0.1875 to 0.1875
- sens_gain: float32 [1024], replicated, may hold values from 0.5 to 1.5
- vid_gain: float32 [1024], replicated, may hold values from 0.5 to 1.5
Outputs:
- sensor_next: bfloat16 [8192, 1024], P(('blk', 'quarter'))
- video_next: bfloat16 [8192, 1024], P(('blk', 'quarter'))
All inputs are finite; a program needn't handle non-finite values.
Results may differ from a plain program's by a relative error of at most 0.0099.
Values may be sent and summed in bfloat16 or wider, within the bound.
A program may use at most 64 MiB of HBM per device.

v0:
```python
import functools
import math

import jax
import jax.numpy as jnp
from jax import lax
from jax.experimental import pallas as pl
from jax.experimental.pallas import tpu as pltpu
from jax.sharding import PartitionSpec as P

H = 16
MESH = pl.DeviceIdType.MESH
F32 = jnp.float32
BF16 = jnp.bfloat16
NX = 4
NY = 4
NP = 16
ROWS = 32
D = 1024
LANES = 128
HEAD = 64
CHUNK = NP * ROWS
TOK = NX * CHUNK
NT = (((1,), (1,)), ((), ()))
C2 = math.log2(math.e) * HEAD ** -0.5
AUG = 80
BLK = 256


def kernel(
    sensor, video, w_sr, w_vr, w_su, w_vu, w_so, w_vo, s_gain, v_gain,
    s_next, v_next,
    wbuf, stage, sb, vb, s_ut, v_ut, num_out, st_out, num_in, st_in, a_out, a_in, sbuf,
    w_sem, z_send, z_recv, g_send, g_recv, n_send, n_recv, t_send, t_recv, r_send, r_recv,
):
    blk = lax.axis_index("blk")
    quarter = lax.axis_index("quarter")
    core = blk % 2
    x_lo = (blk // 2) % 2
    z = blk // 4
    x_hi = quarter % 2
    y = quarter // 2
    x = x_hi * 2 + x_lo
    p = z * 2 + core

    def zc_peer(q):
        return (((q // 2) * 2 + x_lo) * 2 + q % 2, quarter)

    def x_peer(k):
        return ((z * 2 + k % 2) * 2 + core, y * 2 + k // 2)

    def y_peer(k):
        return (blk, k * 2 + x_hi)

    weights = (w_sr, w_su, w_vr, w_vu, w_so, w_vo)
    loads = [pltpu.make_async_copy(w, wbuf.at[k], w_sem.at[k]) for k, w in enumerate(weights)]
    for load in loads:
        load.start()

    barrier = pltpu.get_barrier_semaphore()

    def greet_zc(d, _):
        pl.semaphore_signal(barrier, inc=1, device_id=zc_peer((p + d) % NP), device_id_type=MESH)
        return 0

    def greet_xy(d, _):
        pl.semaphore_signal(barrier, inc=1, device_id=x_peer((x + d) % NX), device_id_type=MESH)
        pl.semaphore_signal(barrier, inc=1, device_id=y_peer((y + d) % NY), device_id_type=MESH)
        return 0

    lax.fori_loop(1, NP, greet_zc, 0)
    lax.fori_loop(1, NX, greet_xy, 0)

    low = lax.broadcasted_iota(jnp.int32, (ROWS, LANES), 1) < HEAD

    def project(rows, first, slot):
        loads[first].wait()
        ref = jnp.dot(rows[...], wbuf[first], preferred_element_type=F32)
        loads[first + 1].wait()
        val = jnp.dot(rows[...], wbuf[first + 1], preferred_element_type=F32)
        for k in range(H // 2):
            a = ref[:, k * LANES:(k + 1) * LANES]
            b = val[:, k * LANES:(k + 1) * LANES]
            stage[slot, 2 * k] = jnp.where(low, a, pltpu.roll(b, HEAD, 1)).astype(BF16)
            stage[slot, 2 * k + 1] = jnp.where(low, pltpu.roll(a, HEAD, 1), b).astype(BF16)

    def send_heads(slot, dst, own):
        def send(d, _):
            q = (p + d) % NP
            pltpu.make_async_remote_copy(
                src_ref=stage.at[slot, q], dst_ref=dst.at[own, p],
                send_sem=z_send.at[slot, q], recv_sem=z_recv.at[slot, p],
                device_id=zc_peer(q), device_id_type=MESH,
            ).start()
            return 0

        lax.fori_loop(1, NP, send, 0)
        dst[own, p] = stage[slot, p]

    def await_heads(slot, dst, own):
        def wait(d, _):
            q = (p + d) % NP
            pltpu.make_async_remote_copy(
                src_ref=stage.at[slot, q], dst_ref=dst.at[own, q],
                send_sem=z_send.at[slot, q], recv_sem=z_recv.at[slot, q],
                device_id=zc_peer(q), device_id_type=MESH,
            ).wait()
            return 0

        lax.fori_loop(1, NP, wait, 0)

    project(sensor, 0, 0)
    pl.semaphore_wait(barrier, (NP - 1) + (NX - 1) + (NY - 1))
    send_heads(0, sb, x)
    project(video, 2, 1)
    send_heads(1, vb, y)

    def gather(slot, buf, own, peer, k):
        return pltpu.make_async_remote_copy(
            src_ref=buf.at[own], dst_ref=buf.at[own],
            send_sem=g_send.at[slot, k], recv_sem=g_recv.at[slot, own],
            device_id=peer(k), device_id_type=MESH,
        )

    def gathered(slot, buf, own, peer, k):
        return pltpu.make_async_remote_copy(
            src_ref=buf.at[own], dst_ref=buf.at[k],
            send_sem=g_send.at[slot, k], recv_sem=g_recv.at[slot, k],
            device_id=peer(k), device_id_type=MESH,
        )

    await_heads(0, sb, x)
    for d in (2, 1, 3):
        gather(0, sb, x, x_peer, (x + d) % NX).start()
    await_heads(1, vb, y)
    for d in (2, 1, 3):
        gather(1, vb, y, y_peer, (y + d) % NY).start()
    for d in (1, 3, 2):
        gathered(0, sb, x, x_peer, (x + d) % NX).wait()
    for d in (1, 3, 2):
        gathered(1, vb, y, y_peer, (y + d) % NY).wait()

    pick = (
        lax.broadcasted_iota(jnp.int32, (AUG, LANES), 1)
        == lax.broadcasted_iota(jnp.int32, (AUG, LANES), 0) + (LANES - AUG)
    )
    ones_row = lax.broadcasted_iota(jnp.int32, (AUG, LANES), 0) < AUG - HEAD
    select = jnp.where(jnp.logical_and(pick, jnp.logical_not(ones_row)), 1.0, 0.0).astype(BF16)

    def transposed(src, dst):
        def part(k, _):
            t = lax.dot_general(
                select, src[k].reshape(CHUNK, LANES), NT, preferred_element_type=F32
            )
            head = lax.broadcasted_iota(jnp.int32, (AUG, CHUNK), 0) < AUG - HEAD
            dst[k] = jnp.where(head, 1.0, t).astype(BF16)
            return 0

        lax.fori_loop(0, NX, part, 0)

    transposed(sb, s_ut)
    transposed(vb, v_ut)

    keep = lax.broadcasted_iota(jnp.int32, (CHUNK, LANES), 1) < HEAD

    def attend(slot, own_side, other_side, other_ut, own, peer):
        def one(d, _):
            k = (own + d) % NX
            mine = jnp.where(
                keep, own_side[k].reshape(CHUNK, LANES), jnp.zeros((), BF16)
            )
            for half in range(CHUNK // BLK):
                cols = slice(half * BLK, (half + 1) * BLK)
                query = mine[cols]
                tops = []
                for j in range(NX):
                    s = lax.dot_general(
                        other_side[j].reshape(CHUNK, LANES), query, NT,
                        preferred_element_type=F32,
                    )
                    sbuf[j] = s
                    tops.append(jnp.max(s, axis=0, keepdims=True))
                top = jnp.maximum(jnp.maximum(tops[0], tops[1]), jnp.maximum(tops[2], tops[3]))
                acc = jnp.zeros((AUG, BLK), F32)
                for j in range(NX):
                    w = jnp.exp2((sbuf[j] - top) * C2).astype(BF16)
                    acc = acc + jnp.dot(other_ut[j], w, preferred_element_type=F32)
                num_out[slot, k, :, cols] = acc[AUG - HEAD:].astype(BF16)
                st_out[slot, k, 0:8, cols] = acc[0:8]
                st_out[slot, k, 8:16, cols] = jnp.broadcast_to(top, (8, BLK))

            @pl.when(d < NX)
            def _():
                pltpu.make_async_remote_copy(
                    src_ref=num_out.at[slot, k], dst_ref=num_in.at[slot, own],
                    send_sem=n_send.at[slot, k], recv_sem=n_recv.at[slot, own],
                    device_id=peer(k), device_id_type=MESH,
                ).start()
                pltpu.make_async_remote_copy(
                    src_ref=st_out.at[slot, k], dst_ref=st_in.at[slot, own],
                    send_sem=t_send.at[slot, k], recv_sem=t_recv.at[slot, own],
                    device_id=peer(k), device_id_type=MESH,
                ).start()

            return 0

        lax.fori_loop(1, NX + 1, one, 0)

    def combine(slot, own, peer):
        for d in (1, 2, 3):
            k = (own + d) % NX
            pltpu.make_async_remote_copy(
                src_ref=num_out.at[slot, k], dst_ref=num_in.at[slot, k],
                send_sem=n_send.at[slot, k], recv_sem=n_recv.at[slot, k],
                device_id=peer(k), device_id_type=MESH,
            ).wait()
            pltpu.make_async_remote_copy(
                src_ref=st_out.at[slot, k], dst_ref=st_in.at[slot, k],
                send_sem=t_send.at[slot, k], recv_sem=t_recv.at[slot, k],
                device_id=peer(k), device_id_type=MESH,
            ).wait()
        num_in[slot, own] = num_out[slot, own]
        st_in[slot, own] = st_out[slot, own]
        tops = [st_in[slot, k, 8:9, :] for k in range(NX)]
        top = jnp.maximum(jnp.maximum(tops[0], tops[1]), jnp.maximum(tops[2], tops[3]))
        total = jnp.zeros((1, CHUNK), F32)
        mixed = jnp.zeros((HEAD, CHUNK), F32)
        for k in range(NX):
            fade = jnp.exp2((tops[k] - top) * C2)
            total = total + st_in[slot, k, 0:1, :] * fade
            mixed = mixed + num_in[slot, k].astype(F32) * fade
        return mixed / total

    attend(0, sb, vb, v_ut, x, x_peer)
    attend(1, vb, sb, s_ut, y, y_peer)
    sens_attn = combine(0, x, x_peer)
    vid_attn = combine(1, y, y_peer)
    both = jnp.concatenate([sens_attn, vid_attn], axis=0)
    a_out[...] = both.T.astype(BF16).reshape(NP, ROWS, LANES)

    def send_back(d, _):
        q = (p + d) % NP
        pltpu.make_async_remote_copy(
            src_ref=a_out.at[q], dst_ref=a_in.at[p],
            send_sem=r_send.at[q], recv_sem=r_recv.at[p],
            device_id=zc_peer(q), device_id_type=MESH,
        ).start()
        return 0

    lax.fori_loop(1, NP, send_back, 0)
    a_in[p] = a_out[p]

    def wait_back(d, _):
        q = (p + d) % NP
        pltpu.make_async_remote_copy(
            src_ref=a_out.at[q], dst_ref=a_in.at[q],
            send_sem=r_send.at[q], recv_sem=r_recv.at[q],
            device_id=zc_peer(q), device_id_type=MESH,
        ).wait()
        return 0

    lax.fori_loop(1, NP, wait_back, 0)

    sens_parts, vid_parts = [], []
    for k in range(H // 2):
        a = a_in[2 * k].astype(F32)
        b = a_in[2 * k + 1].astype(F32)
        sens_parts.append(jnp.where(low, a, pltpu.roll(b, HEAD, 1)))
        vid_parts.append(jnp.where(low, pltpu.roll(a, HEAD, 1), b))

    def finish(rows, parts, gain, slot, out):
        loads[slot].wait()
        mixed = jnp.concatenate(parts, axis=1)
        power = jnp.mean(mixed * mixed, axis=-1, keepdims=True)
        normed = (mixed * lax.rsqrt(power + 1e-6) * gain[...]).astype(BF16)
        update = jnp.dot(normed, wbuf[slot], preferred_element_type=F32)
        out[...] = (rows[...].astype(F32) + update).astype(BF16)

    finish(sensor, sens_parts, s_gain, 4, s_next)
    finish(video, vid_parts, v_gain, 5, v_next)


def local(sensor, video, w_sr, w_vr, w_su, w_vu, w_so, w_vo, s_gain, v_gain):
    vmem = pl.BlockSpec(memory_space=pltpu.VMEM)
    hbm = pl.BlockSpec(memory_space=pl.ANY)
    dma = pltpu.SemaphoreType.DMA
    return pl.pallas_call(
        kernel,
        out_shape=(
            jax.ShapeDtypeStruct(sensor.shape, sensor.dtype),
            jax.ShapeDtypeStruct(video.shape, video.dtype),
        ),
        in_specs=[vmem, vmem] + [hbm] * 6 + [vmem, vmem],
        out_specs=(vmem, vmem),
        scratch_shapes=[
            pltpu.VMEM((6, D, D), BF16),
            pltpu.VMEM((2, NP, ROWS, LANES), BF16),
            pltpu.VMEM((NX, NP, ROWS, LANES), BF16),
            pltpu.VMEM((NY, NP, ROWS, LANES), BF16),
            pltpu.VMEM((NX, AUG, CHUNK), BF16),
            pltpu.VMEM((NY, AUG, CHUNK), BF16),
            pltpu.VMEM((2, NX, HEAD, CHUNK), BF16),
            pltpu.VMEM((2, NX, 16, CHUNK), F32),
            pltpu.VMEM((2, NX, HEAD, CHUNK), BF16),
            pltpu.VMEM((2, NX, 16, CHUNK), F32),
            pltpu.VMEM((NP, ROWS, LANES), BF16),
            pltpu.VMEM((NP, ROWS, LANES), BF16),
            pltpu.VMEM((NX, CHUNK, BLK), F32),
            dma((6,)),
            dma((2, NP)), dma((2, NP)),
            dma((2, NX)), dma((2, NX)),
            dma((2, NX)), dma((2, NX)),
            dma((2, NX)), dma((2, NX)),
            dma((NP,)), dma((NP,)),
        ],
        compiler_params=pltpu.CompilerParams(
            collective_id=0, has_side_effects=True, vmem_limit_bytes=56 * 1024 * 1024
        ),
    )(
        sensor, video, w_sr, w_vr, w_su, w_vu, w_so, w_vo,
        s_gain.reshape(1, D), v_gain.reshape(1, D),
    )


def solution(mesh):
    rows = P(("blk", "quarter"), None)
    return jax.shard_map(
        local,
        mesh=mesh,
        in_specs=(rows, rows) + (P(),) * 8,
        out_specs=(rows, rows),
        check_vma=False,
    )
```

profile of v0, /device:TPU:1, one launch (start us, length us, event | category | flops | bytes accessed | tf_op | source)
XLA Modules:
  0.0 56.4 jit_solution(6983479153718305339)
XLA Ops:
  0.6 52.8 %shard_map.113 = (bf16[32,1024]{1,0:T(8,128)(2,1)}, bf16[32,1024]{1,0:T(8,128)(2,1)}) custom-call(bf16[32,1024]{1,0:T(8,128)(2,1)} %sensor.1, bf16[32,1024]{1,0:T(8,128)(2,1)} %video.1, bf16[1024,1024]{1,0:T(8,128)(2,1)} %w_sr.1, bf16[1024,1024]{1,0:T(8,128)(2,1)} %w_vr.1, bf16[1024,1024]{1,0:T(8,128)(2,1)} %w_su.1, bf16[1024,1024]{1,0:T(8,128)(2,1)} %w_vu.1, ...), custom_call_target="tpu_custom_call" | custom-call | tf_op jit(solution)/shard_map/pallas_call | solution.py:287
  53.5 1.5 %copy.14 = bf16[32,1024]{1,0:T(8,128)(2,1)} copy(bf16[32,1024]{1,0:T(8,128)(2,1)} %get-tuple-element.4) | data formatting | bytes 131072
  55.0 1.5 %copy.15 = bf16[32,1024]{1,0:T(8,128)(2,1)} copy(bf16[32,1024]{1,0:T(8,128)(2,1)} %get-tuple-element.5) | data formatting | bytes 131072
where the time goes:
time: 56.6 us; the launch traced here: 56.4 us
  Pallas kernels  52.8 us (93%)
  local copies, waits for them, and re-layouts  2.95 us (5%)
  between operations  0.64 us (1%)
    pallas_call x1, Pallas kernels, local(): pl.pallas_call(kernel, out_shape=(jax.ShapeDtypeStruct(sensor.shape, sens...  52.8 us
    unnamed x2, local copies, waits for them, and re-layouts  2.95 us

commit v1 on v0

v1 whole, which is shorter than its diff:
```python
import functools
import math

import jax
import jax.numpy as jnp
from jax import lax
from jax.experimental import pallas as pl
from jax.experimental.pallas import tpu as pltpu
from jax.sharding import PartitionSpec as P

H = 16
MESH = pl.DeviceIdType.MESH
F32 = jnp.float32
BF16 = jnp.bfloat16
NX = 4
NY = 4
NP = 16
ROWS = 32
D = 1024
LANES = 128
HEAD = 64
CHUNK = NP * ROWS
TOK = NX * CHUNK
NT = (((1,), (1,)), ((), ()))
C2 = math.log2(math.e) * HEAD ** -0.5
AUG = 80
BLK = 256
HALF = NP // 2


def shift_z(t):
    return (t % 2) * ((t + 1) // 2) - (1 - t % 2) * (t // 2)


def shift_xy(o):
    return o + o // 2 - 2 * (o // 3)


MIRROR = (0, 2, 1, 3)


def kernel(
    sensor, video, w_sr, w_vr, w_su, w_vu, w_so, w_vo, s_gain, v_gain,
    update_out,
    wbuf, stage, chunks, uts, num_out, st_out, num_in, st_in, a_out, a_in, queries, accs, tops, sbuf_a, sbuf_b,
    w_sem, z_send, z_recv, g_send, g_recv, n_send, n_recv, t_send, t_recv, r_send, r_recv,
):
    blk = lax.axis_index("blk")
    quarter = lax.axis_index("quarter")
    core = blk % 2
    x_lo = (blk // 2) % 2
    z = blk // 4
    x_hi = quarter % 2
    y = quarter // 2
    x = x_hi * 2 + x_lo
    p = z * 2 + core

    def zc_peer(q):
        return (((q // 2) * 2 + x_lo) * 2 + q % 2, quarter)

    def x_peer(d):
        k = (x + d) % NX
        return ((z * 2 + k % 2) * 2 + core, y * 2 + k // 2)

    def y_peer(d):
        return (blk, (y + d) % NY * 2 + x_hi)

    peers = (x_peer, y_peer)
    weights = (w_sr, w_su, w_vr, w_vu, w_so, w_vo)
    loads = [pltpu.make_async_copy(w, wbuf.at[k], w_sem.at[k]) for k, w in enumerate(weights)]
    for load in loads:
        load.start()

    barrier = pltpu.get_barrier_semaphore()

    def greet_zc(d, _):
        pl.semaphore_signal(barrier, inc=1, device_id=zc_peer((p + d) % NP), device_id_type=MESH)
        return 0

    def greet_xy(d, _):
        pl.semaphore_signal(barrier, inc=1, device_id=x_peer(d), device_id_type=MESH)
        pl.semaphore_signal(barrier, inc=1, device_id=y_peer(d), device_id_type=MESH)
        return 0

    lax.fori_loop(1, NP, greet_zc, 0)
    lax.fori_loop(1, NX, greet_xy, 0)

    low = lax.broadcasted_iota(jnp.int32, (ROWS, LANES), 1) < HEAD

    def project(rows, first, side):
        loads[first].wait()
        ref = jnp.dot(rows[...], wbuf[first], preferred_element_type=F32)
        loads[first + 1].wait()
        val = jnp.dot(rows[...], wbuf[first + 1], preferred_element_type=F32)
        for k in range(H // 2):
            a = ref[:, k * LANES:(k + 1) * LANES]
            b = val[:, k * LANES:(k + 1) * LANES]
            stage[side, 2 * k] = jnp.where(low, a, pltpu.roll(b, HEAD, 1)).astype(BF16)
            stage[side, 2 * k + 1] = jnp.where(low, pltpu.roll(a, HEAD, 1), b).astype(BF16)

    def head_copy(side, s, sender):
        t = s // 2
        sign = -1 if sender else 1
        q = (z + sign * shift_z(t) + HALF) % HALF * 2 + s % 2
        return pltpu.make_async_remote_copy(
            src_ref=stage.at[side, q],
            dst_ref=chunks.at[side, 0, t * 2 + core if sender else s],
            send_sem=z_send.at[side, s],
            recv_sem=z_recv.at[side, t * 2 + core if sender else s],
            device_id=zc_peer(q), device_id_type=MESH,
        )

    def send_heads(side):
        def send(i, _):
            head_copy(side, (core + 15 - i) % NP, True).start()
            return 0

        lax.fori_loop(0, NP - 1, send, 0)
        chunks[side, 0, core] = stage[side, p]

    def await_heads(side, group):
        def wait(d, _):
            s = (core + d) % HALF if group == 0 else HALF + d
            head_copy(side, s, False).wait()
            return 0

        lax.fori_loop(1 if group == 0 else 0, HALF, wait, 0)

    def gather_copy(side, group, o):
        part = pl.ds(group * HALF, HALF)
        return pltpu.make_async_remote_copy(
            src_ref=chunks.at[side, 0, part], dst_ref=chunks.at[side, MIRROR[o], part],
            send_sem=g_send.at[side, group, o], recv_sem=g_recv.at[side, group, MIRROR[o]],
            device_id=peers[side](shift_xy(o)), device_id_type=MESH,
        )

    def gathered(side, group, o):
        part = pl.ds(group * HALF, HALF)
        return pltpu.make_async_remote_copy(
            src_ref=chunks.at[side, 0, part], dst_ref=chunks.at[side, o, part],
            send_sem=g_send.at[side, group, o], recv_sem=g_recv.at[side, group, o],
            device_id=peers[side](shift_xy(o)), device_id_type=MESH,
        )

    project(sensor, 0, 0)
    pl.semaphore_wait(barrier, (NP - 1) + (NX - 1) + (NY - 1))
    send_heads(0)
    project(video, 2, 1)
    send_heads(1)
    for group in range(2):
        for side in range(2):
            await_heads(side, group)
            for o in (1, 2):
                gather_copy(side, group, o).start()
    for group in range(2):
        for side in range(2):
            gather_copy(side, group, 3).start()

    head_rows = lax.broadcasted_iota(jnp.int32, (AUG, LANES), 0) < AUG - HEAD
    pick = (
        lax.broadcasted_iota(jnp.int32, (AUG, LANES), 1)
        == lax.broadcasted_iota(jnp.int32, (AUG, LANES), 0) + (LANES - AUG)
    )
    select = jnp.where(jnp.logical_and(pick, jnp.logical_not(head_rows)), 1.0, 0.0).astype(BF16)
    top_rows = lax.broadcasted_iota(jnp.int32, (AUG, CHUNK), 0) < AUG - HEAD
    keep = lax.broadcasted_iota(jnp.int32, (CHUNK, LANES), 1) < HEAD

    def chunk(side, o):
        return chunks[side, o].reshape(CHUNK, LANES)

    def prepare(side, o):
        t = lax.dot_general(select, chunk(side, o), NT, preferred_element_type=F32)
        uts[side, o] = jnp.where(top_rows, 1.0, t).astype(BF16)
        queries[side, o] = jnp.where(keep, chunk(side, o), jnp.zeros((), BF16))

    def scores(side, mine, half, others, buf):
        query = queries[side, mine, half * BLK:(half + 1) * BLK]
        top = None
        for k, other in enumerate(others):
            s = lax.dot_general(chunk(1 - side, other), query, NT, preferred_element_type=F32)
            buf[k] = s
            t = jnp.max(s, axis=0, keepdims=True)
            top = t if top is None else jnp.maximum(top, t)
        return top

    def weigh(side, mine, half, others, buf, top, fresh):
        cols = slice(half * BLK, (half + 1) * BLK)
        acc = None
        if not fresh:
            old = tops[side, mine, 0:1, cols]
            top = jnp.maximum(top, old)
            acc = accs[side, mine, :, cols] * jnp.exp2((old - top) * C2)
        for k, other in enumerate(others):
            w = jnp.exp2((buf[k] - top) * C2).astype(BF16)
            term = jnp.dot(uts[1 - side, other], w, preferred_element_type=F32)
            acc = term if acc is None else acc + term
        return acc, top

    def publish(side, o):
        there = MIRROR[o]
        pltpu.make_async_remote_copy(
            src_ref=num_out.at[side, o], dst_ref=num_in.at[side, there],
            send_sem=n_send.at[side, o], recv_sem=n_recv.at[side, there],
            device_id=peers[side](shift_xy(o)), device_id_type=MESH,
        ).start()
        pltpu.make_async_remote_copy(
            src_ref=st_out.at[side, o], dst_ref=st_in.at[side, there],
            send_sem=t_send.at[side, o], recv_sem=t_recv.at[side, there],
            device_id=peers[side](shift_xy(o)), device_id_type=MESH,
        ).start()

    def store(side, mine, half, acc, top, last):
        cols = slice(half * BLK, (half + 1) * BLK)
        if last:
            num_out[side, mine, :, cols] = acc[AUG - HEAD:].astype(BF16)
            st_out[side, mine, 0:8, cols] = acc[0:8]
            st_out[side, mine, 8:16, cols] = jnp.broadcast_to(top, (8, BLK))
            if mine and half:
                publish(side, mine)
        else:
            accs[side, mine, :, cols] = acc
            tops[side, mine, :, cols] = jnp.broadcast_to(top, (8, BLK))

    bufs = (sbuf_a, sbuf_b)
    for wave in range(NX):
        if wave:
            for group in range(2):
                for side in range(2):
                    gathered(side, group, wave).wait()
        prepare(0, wave)
        prepare(1, wave)
        last = wave == NX - 1
        units = []
        for side in range(2):
            for mine in range(1, wave):
                units += [(side, mine, half, (wave,)) for half in range(2)]
            units += [(side, wave, half, tuple(range(wave + 1))) for half in range(2)]
        if wave:
            units += [(side, 0, half, (wave,)) for side in range(2) for half in range(2)]
        top = scores(*units[0], bufs[0])
        for n, unit in enumerate(units):
            following = None
            if n + 1 < len(units):
                following = scores(*units[n + 1], bufs[(n + 1) % 2])
            acc, top = weigh(*unit, bufs[n % 2], top, unit[1] == wave)
            store(*unit[:3], acc, top, last)
            top = following

    def combine(side):
        for o in (1, 2, 3):
            pltpu.make_async_remote_copy(
                src_ref=num_out.at[side, o], dst_ref=num_in.at[side, o],
                send_sem=n_send.at[side, o], recv_sem=n_recv.at[side, o],
                device_id=peers[side](shift_xy(o)), device_id_type=MESH,
            ).wait()
            pltpu.make_async_remote_copy(
                src_ref=st_out.at[side, o], dst_ref=st_in.at[side, o],
                send_sem=t_send.at[side, o], recv_sem=t_recv.at[side, o],
                device_id=peers[side](shift_xy(o)), device_id_type=MESH,
            ).wait()
        nums = [num_out[side, 0]] + [num_in[side, o] for o in (1, 2, 3)]
        stats = [st_out[side, 0]] + [st_in[side, o] for o in (1, 2, 3)]
        highs = [s[8:9] for s in stats]
        top = jnp.maximum(jnp.maximum(highs[0], highs[1]), jnp.maximum(highs[2], highs[3]))
        total = jnp.zeros((1, CHUNK), F32)
        mixed = jnp.zeros((HEAD, CHUNK), F32)
        for o in range(NX):
            fade = jnp.exp2((highs[o] - top) * C2)
            total = total + stats[o][0:1] * fade
            mixed = mixed + nums[o].astype(F32) * fade
        attn = mixed / total
        pair = jnp.concatenate([attn, pltpu.roll(attn, CHUNK - ROWS // 2, 1)], axis=0)
        a_out[side] = pair.T.astype(BF16).reshape(NP, ROWS, LANES)[:, :ROWS // 2]

        def send_back(d, _):
            s = (core + d) % NP
            q = (z + shift_z(s // 2) + HALF) % HALF * 2 + s % 2
            pltpu.make_async_remote_copy(
                src_ref=a_out.at[side, s], dst_ref=a_in.at[side, p],
                send_sem=r_send.at[side, q], recv_sem=r_recv.at[side, p],
                device_id=zc_peer(q), device_id_type=MESH,
            ).start()
            return 0

        lax.fori_loop(1, NP, send_back, 0)
        a_in[side, p] = a_out[side, core]

    def wait_back(side):
        def wait(d, _):
            q = (p + d) % NP
            pltpu.make_async_remote_copy(
                src_ref=a_out.at[side, 0], dst_ref=a_in.at[side, q],
                send_sem=r_send.at[side, q], recv_sem=r_recv.at[side, q],
                device_id=zc_peer(q), device_id_type=MESH,
            ).wait()
            return 0

        lax.fori_loop(1, NP, wait, 0)

    half_low = low[:ROWS // 2]

    def finish(side, gain):
        wait_back(side)
        parts = []
        for k in range(H // 2):
            a = a_in[side, 2 * k].astype(F32)
            b = a_in[side, 2 * k + 1].astype(F32)
            upper = jnp.where(half_low, a, pltpu.roll(b, HEAD, 1))
            lower = jnp.where(half_low, pltpu.roll(a, HEAD, 1), b)
            parts.append(jnp.concatenate([upper, lower], axis=0))
        mixed = jnp.concatenate(parts, axis=1)
        power = jnp.mean(mixed * mixed, axis=-1, keepdims=True)
        normed = (mixed * lax.rsqrt(power + 1e-6) * gain[...]).astype(BF16)
        update = jnp.dot(normed, wbuf[4 + side], preferred_element_type=F32)
        update_out[side * ROWS:(side + 1) * ROWS] = update

    combine(0)
    loads[4].wait()
    loads[5].wait()
    combine(1)
    finish(0, s_gain)
    finish(1, v_gain)


def local(sensor, video, w_sr, w_vr, w_su, w_vu, w_so, w_vo, s_gain, v_gain):
    vmem = pl.BlockSpec(memory_space=pltpu.VMEM)
    hbm = pl.BlockSpec(memory_space=pl.ANY)
    dma = pltpu.SemaphoreType.DMA
    update = pl.pallas_call(
        kernel,
        out_shape=jax.ShapeDtypeStruct((2 * ROWS, D), F32),
        in_specs=[vmem, vmem] + [hbm] * 6 + [vmem, vmem],
        out_specs=vmem,
        scratch_shapes=[
            pltpu.VMEM((6, D, D), BF16),
            pltpu.VMEM((2, NP, ROWS, LANES), BF16),
            pltpu.VMEM((2, NX, NP, ROWS, LANES), BF16),
            pltpu.VMEM((2, NX, AUG, CHUNK), BF16),
            pltpu.VMEM((2, NX, HEAD, CHUNK), BF16),
            pltpu.VMEM((2, NX, 16, CHUNK), F32),
            pltpu.VMEM((2, NX, HEAD, CHUNK), BF16),
            pltpu.VMEM((2, NX, 16, CHUNK), F32),
            pltpu.VMEM((2, NP, ROWS // 2, LANES), BF16),
            pltpu.VMEM((2, NP, ROWS // 2, LANES), BF16),
            pltpu.VMEM((2, NX, CHUNK, LANES), BF16),
            pltpu.VMEM((2, NX, AUG, CHUNK), F32),
            pltpu.VMEM((2, NX, 8, CHUNK), F32),
            pltpu.VMEM((NX, CHUNK, BLK), F32),
            pltpu.VMEM((NX, CHUNK, BLK), F32),
            dma((6,)),
            dma((2, NP)), dma((2, NP)),
            dma((2, 2, NX)), dma((2, 2, NX)),
            dma((2, NX)), dma((2, NX)),
            dma((2, NX)), dma((2, NX)),
            dma((2, NP)), dma((2, NP)),
        ],
        compiler_params=pltpu.CompilerParams(
            collective_id=0, has_side_effects=True, vmem_limit_bytes=60 * 1024 * 1024
        ),
    )(
        sensor, video, w_sr, w_vr, w_su, w_vu, w_so, w_vo,
        s_gain.reshape(1, D), v_gain.reshape(1, D),
    )
    return (
        (sensor.astype(F32) + update[:ROWS]).astype(BF16),
        (video.astype(F32) + update[ROWS:]).astype(BF16),
    )


def solution(mesh):
    rows = P(("blk", "quarter"), None)
    return jax.shard_map(
        local,
        mesh=mesh,
        in_specs=(rows, rows) + (P(),) * 8,
        out_specs=(rows, rows),
        check_vma=False,
    )
```

time: 56.6 us -> 51.9 us (0.917)
  Pallas kernels: 52.8 us -> 49.4 us
  local copies, waits for them, and re-layouts: 2.95 us -> 0.01 us
  other arithmetic: 0 us -> 1.65 us
    pallas_call x1, Pallas kernels: 52.8 us -> 49.4 us  [local(): pl.pallas_call(kernel, out_shape=jax.ShapeDtypeStruct((2 * ROWS, D), F32)...]
    unnamed x2 -> x4, local copies, waits for them, and re-layouts: 2.95 us -> 0.01 us
    convert_element_type x0 -> x1, other arithmetic: none -> 1.65 us  [local(): (video.astype(F32) + update[ROWS:]).astype(BF16)]
where the time goes in v1:
time: 51.9 us; the launch traced here: 51.7 us
  Pallas kernels  49.4 us (95%)
  other arithmetic  1.65 us (3%)
  between operations  0.67 us (1%)
    pallas_call x1, Pallas kernels, local(): pl.pallas_call(kernel, out_shape=jax.ShapeDtypeStruct((2 * ROWS, D), F32)...  49.4 us
    convert_element_type x1, other arithmetic, local(): (video.astype(F32) + update[ROWS:]).astype(BF16)  1.65 us

profile of v1, /device:TPU:1, one launch (start us, length us, event | category | flops | bytes accessed | tf_op | source)
XLA Modules:
  0.0 51.7 jit_solution(7121717105474932943)
XLA Ops:
  0.6 0.0 copy-start
  0.6 0.0 copy-start.1
  0.7 49.4 %shard_map.113 = f32[64,1024]{1,0:T(8,128)} custom-call(bf16[32,1024]{1,0:T(8,128)(2,1)} %sensor.1, bf16[32,1024]{1,0:T(8,128)(2,1)} %video.1, bf16[1024,1024]{1,0:T(8,128)(2,1)} %w_sr.1, bf16[1024,1024]{1,0:T(8,128)(2,1)} %w_vr.1, bf16[1024,1024]{1,0:T(8,128)(2,1)} %w_su.1, bf16[1024,1024]{1,0:T(8,128)(2,1)} %w_vu.1, bf16[1024,1024]{1,0:T(8,128)(2,1)} %w_so.1, ...), custom_call_target="tpu_custom_call" | custom-call | tf_op jit(solution)/shard_map/pallas_call | solution.py:329
  50.0 0.0 copy-done
  50.1 0.0 copy-done.1
  50.1 1.6 %add_convert_fusion = (bf16[32,1024]{1,0:T(8,128)(2,1)}, bf16[32,1024]{1,0:T(8,128)(2,1)}) fusion(f32[64,1024]{1,0:T(8,128)} %shard_map.113, bf16[32,1024]{1,0:T(8,128)(2,1)S(1)} %copy-done.1, bf16[32,1024]{1,0:T(8,128)(2,1)S(1)} %copy-done), kind=kLoop, calls=%fused_computation | loop fusion | flops 196608 | bytes 524288 | tf_op jit(solution)/shard_map/convert_element_type | solution.py:366
Async XLA Ops:
  0.6 49.4 %copy-start = (bf16[32,1024]{1,0:T(8,128)(2,1)S(1)}, bf16[32,1024]{1,0:T(8,128)(2,1)}, u32[]{:S(2)}) copy-start(bf16[32,1024]{1,0:T(8,128)(2,1)} %sensor.1) | copy-start | bytes 196612
  0.6 49.4 %copy-start.1 = (bf16[32,1024]{1,0:T(8,128)(2,1)S(1)}, bf16[32,1024]{1,0:T(8,128)(2,1)}, u32[]{:S(2)}) copy-start(bf16[32,1024]{1,0:T(8,128)(2,1)} %video.1) | copy-start | bytes 196612

commit v2 on v1

--- a/solution.py
+++ b/solution.py
@@ -26,6 +26,7 @@
 AUG = 80
 BLK = 256
 HALF = NP // 2
+GROUPS = ((0, 8), (8, 4), (12, 4))
 
 
 def shift_z(t):
@@ -42,7 +43,7 @@
 def kernel(
     sensor, video, w_sr, w_vr, w_su, w_vu, w_so, w_vo, s_gain, v_gain,
     update_out,
-    wbuf, stage, chunks, uts, num_out, st_out, num_in, st_in, a_out, a_in, queries, accs, tops, sbuf_a, sbuf_b,
+    wbuf, stage, chunks, s_ut, num_out, st_out, num_in, st_in, a_out, a_in, v_ref, v_val, v_acc, v_top, s_acc, s_top, sbuf_a, sbuf_b, k0, k1, k2, k3, k4, k5,
     w_sem, z_send, z_recv, g_send, g_recv, n_send, n_recv, t_send, t_recv, r_send, r_recv,
 ):
     blk = lax.axis_index("blk")
@@ -110,24 +111,28 @@
             device_id=zc_peer(q), device_id_type=MESH,
         )
 
-    def send_heads(side):
-        def send(i, _):
-            head_copy(side, (core + 15 - i) % NP, True).start()
+    def send_heads(side, group):
+        def send(d, _):
+            first, size = GROUPS[group]
+            s = (core + d) % size if group == 0 else first + d
+            head_copy(side, s, True).start()
             return 0
 
-        lax.fori_loop(0, NP - 1, send, 0)
-        chunks[side, 0, core] = stage[side, p]
+        lax.fori_loop(1 if group == 0 else 0, GROUPS[group][1], send, 0)
+        if group == 0:
+            chunks[side, 0, core] = stage[side, p]
 
     def await_heads(side, group):
         def wait(d, _):
-            s = (core + d) % HALF if group == 0 else HALF + d
+            first, size = GROUPS[group]
+            s = (core + d) % size if group == 0 else first + d
             head_copy(side, s, False).wait()
             return 0
 
-        lax.fori_loop(1 if group == 0 else 0, HALF, wait, 0)
+        lax.fori_loop(1 if group == 0 else 0, GROUPS[group][1], wait, 0)
 
     def gather_copy(side, group, o):
-        part = pl.ds(group * HALF, HALF)
+        part = pl.ds(*GROUPS[group])
         return pltpu.make_async_remote_copy(
             src_ref=chunks.at[side, 0, part], dst_ref=chunks.at[side, MIRROR[o], part],
             send_sem=g_send.at[side, group, o], recv_sem=g_recv.at[side, group, MIRROR[o]],
@@ -135,7 +140,7 @@
         )
 
     def gathered(side, group, o):
-        part = pl.ds(group * HALF, HALF)
+        part = pl.ds(*GROUPS[group])
         return pltpu.make_async_remote_copy(
             src_ref=chunks.at[side, 0, part], dst_ref=chunks.at[side, o, part],
             send_sem=g_send.at[side, group, o], recv_sem=g_recv.at[side, group, o],
@@ -143,16 +148,17 @@
         )
 
     project(sensor, 0, 0)
+    project(video, 2, 1)
     pl.semaphore_wait(barrier, (NP - 1) + (NX - 1) + (NY - 1))
-    send_heads(0)
-    project(video, 2, 1)
-    send_heads(1)
-    for group in range(2):
+    for group in range(len(GROUPS)):
+        for side in range(2):
+            send_heads(side, group)
+    for group in range(len(GROUPS)):
         for side in range(2):
             await_heads(side, group)
             for o in (1, 2):
                 gather_copy(side, group, o).start()
-    for group in range(2):
+    for group in range(len(GROUPS)):
         for side in range(2):
             gather_copy(side, group, 3).start()
 
@@ -168,33 +174,24 @@
     def chunk(side, o):
         return chunks[side, o].reshape(CHUNK, LANES)
 
-    def prepare(side, o):
-        t = lax.dot_general(select, chunk(side, o), NT, preferred_element_type=F32)
-        uts[side, o] = jnp.where(top_rows, 1.0, t).astype(BF16)
-        queries[side, o] = jnp.where(keep, chunk(side, o), jnp.zeros((), BF16))
-
-    def scores(side, mine, half, others, buf):
-        query = queries[side, mine, half * BLK:(half + 1) * BLK]
-        top = None
-        for k, other in enumerate(others):
-            s = lax.dot_general(chunk(1 - side, other), query, NT, preferred_element_type=F32)
-            buf[k] = s
-            t = jnp.max(s, axis=0, keepdims=True)
-            top = t if top is None else jnp.maximum(top, t)
-        return top
-
-    def weigh(side, mine, half, others, buf, top, fresh):
-        cols = slice(half * BLK, (half + 1) * BLK)
-        acc = None
-        if not fresh:
-            old = tops[side, mine, 0:1, cols]
-            top = jnp.maximum(top, old)
-            acc = accs[side, mine, :, cols] * jnp.exp2((old - top) * C2)
-        for k, other in enumerate(others):
-            w = jnp.exp2((buf[k] - top) * C2).astype(BF16)
-            term = jnp.dot(uts[1 - side, other], w, preferred_element_type=F32)
-            acc = term if acc is None else acc + term
-        return acc, top
+    def prepare(o):
+        t = lax.dot_general(select, chunk(0, o), NT, preferred_element_type=F32)
+        s_ut[o] = jnp.where(top_rows, 1.0, t).astype(BF16)
+        v_ref[o] = jnp.where(keep, chunk(1, o), jnp.zeros((), BF16))
+        v_val[o] = jnp.where(keep, jnp.ones((), BF16), chunk(1, o))
+
+    halves = [slice(half * BLK, (half + 1) * BLK) for half in range(CHUNK // BLK)]
+
+    def scores(a, b, buf):
+        cols, rows = [], None
+        for n, part in enumerate(halves):
+            s = lax.dot_general(chunk(0, a), v_ref[b, part], NT, preferred_element_type=F32)
+            buf[n] = s
+            cols.append(jnp.max(s, axis=0, keepdims=True))
+            r = jnp.maximum(s[:, :LANES], s[:, LANES:])
+            rows = r if rows is None else jnp.maximum(rows, r)
+        rows = jnp.broadcast_to(jnp.max(rows, axis=1, keepdims=True), (CHUNK, LANES))
+        return cols, rows
 
     def publish(side, o):
         there = MIRROR[o]
@@ -209,42 +206,86 @@
             device_id=peers[side](shift_xy(o)), device_id_type=MESH,
         ).start()
 
-    def store(side, mine, half, acc, top, last):
-        cols = slice(half * BLK, (half + 1) * BLK)
+    first_row = lax.broadcasted_iota(jnp.int32, (8, BLK), 0) == 0
+    top_lane = lax.broadcasted_iota(jnp.int32, (CHUNK, LANES), 1) == 1
+
+    def weigh_video(a, b, buf, cols, fresh, last):
+        for n, part in enumerate(halves):
+            top = cols[n]
+            if not fresh:
+                old = v_top[b, 0:1, part]
+                top = jnp.maximum(top, old)
+            w = jnp.exp2((buf[n] - top) * C2).astype(BF16)
+            acc = jnp.dot(s_ut[a], w, preferred_element_type=F32)
+            if not fresh:
+                acc = acc + v_acc[b, :, part] * jnp.exp2((old - top) * C2)
+            if last:
+                num_out[1, b, :, part] = acc[AUG - HEAD:].astype(BF16)
+                st_out[1, b, :, part] = jnp.where(first_row, acc[0:8], top)
+            else:
+                v_acc[b, :, part] = acc
+                v_top[b, :, part] = jnp.broadcast_to(top, (8, BLK))
+        if last and b:
+            publish(1, b)
+
+    def weigh_sensor(a, b, buf, top, fresh, last):
+        if not fresh:
+            old = s_top[a]
+            top = jnp.maximum(top, old)
+        wide = jnp.concatenate([top] * (BLK // LANES), axis=1)
+        acc = None
+        for n, part in enumerate(halves):
+            w = jnp.exp2((buf[n] - wide) * C2).astype(BF16)
+            term = jnp.dot(w, v_val[b, part], preferred_element_type=F32)
+            acc = term if acc is None else acc + term
+        if not fresh:
+            acc = acc + s_acc[a] * jnp.exp2((old - top) * C2)
         if last:
-            num_out[side, mine, :, cols] = acc[AUG - HEAD:].astype(BF16)
-            st_out[side, mine, 0:8, cols] = acc[0:8]
-            st_out[side, mine, 8:16, cols] = jnp.broadcast_to(top, (8, BLK))
-            if mine and half:
-                publish(side, mine)
+            t = jnp.where(top_lane, top, acc).T
+            num_out[0, a] = t[HEAD:].astype(BF16)
+            st_out[0, a] = t[:8]
+            if a:
+                publish(0, a)
         else:
-            accs[side, mine, :, cols] = acc
-            tops[side, mine, :, cols] = jnp.broadcast_to(top, (8, BLK))
+            s_acc[a] = acc
+            s_top[a] = top
 
     bufs = (sbuf_a, sbuf_b)
+    kept = (k0, k1, k2, k3, k4, k5)
+    later = []
+    s_count, v_count = [0] * NX, [0] * NX
     for wave in range(NX):
         if wave:
-            for group in range(2):
+            for group in range(len(GROUPS)):
                 for side in range(2):
                     gathered(side, group, wave).wait()
-        prepare(0, wave)
-        prepare(1, wave)
-        last = wave == NX - 1
-        units = []
-        for side in range(2):
-            for mine in range(1, wave):
-                units += [(side, mine, half, (wave,)) for half in range(2)]
-            units += [(side, wave, half, tuple(range(wave + 1))) for half in range(2)]
-        if wave:
-            units += [(side, 0, half, (wave,)) for side in range(2) for half in range(2)]
-        top = scores(*units[0], bufs[0])
-        for n, unit in enumerate(units):
+        prepare(wave)
+        tiles = []
+        for o in list(range(1, wave)) + ([0] if wave else []):
+            tiles += [(wave, o), (o, wave)]
+        tiles.append((wave, wave))
+        places = []
+        for n, (a, b) in enumerate(tiles):
+            own = (a == 0) != (b == 0)
+            places.append(kept[2 * (a + b - 1) + (a == 0)] if own else bufs[n % 2])
+        tops = scores(*tiles[0], places[0])
+        for n, (a, b) in enumerate(tiles):
             following = None
-            if n + 1 < len(units):
-                following = scores(*units[n + 1], bufs[(n + 1) % 2])
-            acc, top = weigh(*unit, bufs[n % 2], top, unit[1] == wave)
-            store(*unit[:3], acc, top, last)
-            top = following
+            if n + 1 < len(tiles):
+                following = scores(*tiles[n + 1], places[n + 1])
+            if b or not a:
+                weigh_video(a, b, places[n], tops[0], v_count[b] == 0, v_count[b] == NX - 1)
+                v_count[b] += 1
+            else:
+                later.append((weigh_video, a, b, places[n], tops[0]))
+            if a or not b:
+                weigh_sensor(a, b, places[n], tops[1], s_count[a] == 0, s_count[a] == NX - 1)
+                s_count[a] += 1
+            else:
+                later.append((weigh_sensor, a, b, places[n], tops[1]))
+            tops = following
+    for part, a, b, place, top in later:
+        part(a, b, place, top, False, a + b == NX - 1)
 
     def combine(side):
         for o in (1, 2, 3):
@@ -260,7 +301,7 @@
             ).wait()
         nums = [num_out[side, 0]] + [num_in[side, o] for o in (1, 2, 3)]
         stats = [st_out[side, 0]] + [st_in[side, o] for o in (1, 2, 3)]
-        highs = [s[8:9] for s in stats]
+        highs = [s[1:2] for s in stats]
         top = jnp.maximum(jnp.maximum(highs[0], highs[1]), jnp.maximum(highs[2], highs[3]))
         total = jnp.zeros((1, CHUNK), F32)
         mixed = jnp.zeros((HEAD, CHUNK), F32)
@@ -273,7 +314,7 @@
         a_out[side] = pair.T.astype(BF16).reshape(NP, ROWS, LANES)[:, :ROWS // 2]
 
         def send_back(d, _):
-            s = (core + d) % NP
+            s = (core + NP - d) % NP
             q = (z + shift_z(s // 2) + HALF) % HALF * 2 + s % 2
             pltpu.make_async_remote_copy(
                 src_ref=a_out.at[side, s], dst_ref=a_in.at[side, p],
@@ -335,21 +376,30 @@
             pltpu.VMEM((6, D, D), BF16),
             pltpu.VMEM((2, NP, ROWS, LANES), BF16),
             pltpu.VMEM((2, NX, NP, ROWS, LANES), BF16),
-            pltpu.VMEM((2, NX, AUG, CHUNK), BF16),
+            pltpu.VMEM((NX, AUG, CHUNK), BF16),
             pltpu.VMEM((2, NX, HEAD, CHUNK), BF16),
-            pltpu.VMEM((2, NX, 16, CHUNK), F32),
+            pltpu.VMEM((2, NX, 8, CHUNK), F32),
             pltpu.VMEM((2, NX, HEAD, CHUNK), BF16),
-            pltpu.VMEM((2, NX, 16, CHUNK), F32),
+            pltpu.VMEM((2, NX, 8, CHUNK), F32),
             pltpu.VMEM((2, NP, ROWS // 2, LANES), BF16),
             pltpu.VMEM((2, NP, ROWS // 2, LANES), BF16),
-            pltpu.VMEM((2, NX, CHUNK, LANES), BF16),
-            pltpu.VMEM((2, NX, AUG, CHUNK), F32),
-            pltpu.VMEM((2, NX, 8, CHUNK), F32),
-            pltpu.VMEM((NX, CHUNK, BLK), F32),
-            pltpu.VMEM((NX, CHUNK, BLK), F32),
+            pltpu.VMEM((NX, CHUNK, LANES), BF16),
+            pltpu.VMEM((NX, CHUNK, LANES), BF16),
+            pltpu.VMEM((NX, AUG, CHUNK), F32),
+            pltpu.VMEM((NX, 8, CHUNK), F32),
+            pltpu.VMEM((NX, CHUNK, LANES), F32),
+            pltpu.VMEM((NX, CHUNK, LANES), F32),
+            pltpu.VMEM((2, CHUNK, BLK), F32),
+            pltpu.VMEM((2, CHUNK, BLK), F32),
+            pltpu.VMEM((2, CHUNK, BLK), F32),
+            pltpu.VMEM((2, CHUNK, BLK), F32),
+            pltpu.VMEM((2, CHUNK, BLK), F32),
+            pltpu.VMEM((2, CHUNK, BLK), F32),
+            pltpu.VMEM((2, CHUNK, BLK), F32),
+            pltpu.VMEM((2, CHUNK, BLK), F32),
             dma((6,)),
             dma((2, NP)), dma((2, NP)),
-            dma((2, 2, NX)), dma((2, 2, NX)),
+            dma((2, len(GROUPS), NX)), dma((2, len(GROUPS), NX)),
             dma((2, NX)), dma((2, NX)),
             dma((2, NX)), dma((2, NX)),
             dma((2, NP)), dma((2, NP)),

time: 51.9 us -> 47.9 us (0.923)
  Pallas kernels: 49.4 us -> 45.4 us
    pallas_call x1, Pallas kernels: 49.4 us -> 45.4 us  [local(): pl.pallas_call(kernel, out_shape=jax.ShapeDtypeStruct((2 * ROWS, D), F32)...]
where the time goes in v2:
time: 47.9 us; the launch traced here: 47.7 us
  Pallas kernels  45.4 us (95%)
  other arithmetic  1.65 us (3%)
  between operations  0.67 us (1%)
    pallas_call x1, Pallas kernels, local(): pl.pallas_call(kernel, out_shape=jax.ShapeDtypeStruct((2 * ROWS, D), F32)...  45.4 us
    convert_element_type x1, other arithmetic, local(): (video.astype(F32) + update[ROWS:]).astype(BF16)  1.65 us

profile of v2, /device:TPU:1, one launch (start us, length us, event | category | flops | bytes accessed | tf_op | source)
XLA Modules:
  0.0 47.7 jit_solution(15146663267563705752)
XLA Ops:
  0.6 0.0 copy-start
  0.6 0.0 copy-start.1
  0.7 45.4 %shard_map.113 = f32[64,1024]{1,0:T(8,128)} custom-call(bf16[32,1024]{1,0:T(8,128)(2,1)} %sensor.1, bf16[32,1024]{1,0:T(8,128)(2,1)} %video.1, bf16[1024,1024]{1,0:T(8,128)(2,1)} %w_sr.1, bf16[1024,1024]{1,0:T(8,128)(2,1)} %w_vr.1, bf16[1024,1024]{1,0:T(8,128)(2,1)} %w_su.1, bf16[1024,1024]{1,0:T(8,128)(2,1)} %w_vu.1, bf16[1024,1024]{1,0:T(8,128)(2,1)} %w_so.1, ...), custom_call_target="tpu_custom_call" | custom-call | tf_op jit(solution)/shard_map/pallas_call | solution.py:370
  46.1 0.0 copy-done
  46.1 0.0 copy-done.1
  46.1 1.6 %add_convert_fusion = (bf16[32,1024]{1,0:T(8,128)(2,1)}, bf16[32,1024]{1,0:T(8,128)(2,1)}) fusion(f32[64,1024]{1,0:T(8,128)} %shard_map.113, bf16[32,1024]{1,0:T(8,128)(2,1)S(1)} %copy-done.1, bf16[32,1024]{1,0:T(8,128)(2,1)S(1)} %copy-done), kind=kLoop, calls=%fused_computation | loop fusion | flops 196608 | bytes 524288 | tf_op jit(solution)/shard_map/convert_element_type | solution.py:416
Async XLA Ops:
  0.6 45.4 %copy-start = (bf16[32,1024]{1,0:T(8,128)(2,1)S(1)}, bf16[32,1024]{1,0:T(8,128)(2,1)}, u32[]{:S(2)}) copy-start(bf16[32,1024]{1,0:T(8,128)(2,1)} %sensor.1) | copy-start | bytes 196612
  0.6 45.4 %copy-start.1 = (bf16[32,1024]{1,0:T(8,128)(2,1)S(1)}, bf16[32,1024]{1,0:T(8,128)(2,1)}, u32[]{:S(2)}) copy-start(bf16[32,1024]{1,0:T(8,128)(2,1)} %video.1) | copy-start | bytes 196612

commit v3 on v2

--- a/solution.py
+++ b/solution.py
@@ -102,23 +102,22 @@
     def head_copy(side, s, sender):
         t = s // 2
         sign = -1 if sender else 1
-        q = (z + sign * shift_z(t) + HALF) % HALF * 2 + s % 2
+        there = (z + sign * shift_z(t) + HALF) % HALF
+        q = there * 2 + s % 2
         return pltpu.make_async_remote_copy(
             src_ref=stage.at[side, q],
             dst_ref=chunks.at[side, 0, t * 2 + core if sender else s],
             send_sem=z_send.at[side, s],
             recv_sem=z_recv.at[side, t * 2 + core if sender else s],
-            device_id=zc_peer(q), device_id_type=MESH,
+            device_id=(there * 4 + x_lo * 2 + s % 2, quarter), device_id_type=MESH,
         )
 
     def send_heads(side, group):
-        def send(d, _):
-            first, size = GROUPS[group]
-            s = (core + d) % size if group == 0 else first + d
+        first, size = GROUPS[group]
+        if group == 0:
+            head_copy(side, 1 - core, True).start()
+        for s in range(2 if group == 0 else first, first + size):
             head_copy(side, s, True).start()
-            return 0
-
-        lax.fori_loop(1 if group == 0 else 0, GROUPS[group][1], send, 0)
         if group == 0:
             chunks[side, 0, core] = stage[side, p]
 
@@ -206,7 +205,6 @@
             device_id=peers[side](shift_xy(o)), device_id_type=MESH,
         ).start()
 
-    first_row = lax.broadcasted_iota(jnp.int32, (8, BLK), 0) == 0
     top_lane = lax.broadcasted_iota(jnp.int32, (CHUNK, LANES), 1) == 1
 
     def weigh_video(a, b, buf, cols, fresh, last):
@@ -221,7 +219,10 @@
                 acc = acc + v_acc[b, :, part] * jnp.exp2((old - top) * C2)
             if last:
                 num_out[1, b, :, part] = acc[AUG - HEAD:].astype(BF16)
-                st_out[1, b, :, part] = jnp.where(first_row, acc[0:8], top)
+                for k in range(BLK // LANES):
+                    row = n * (BLK // LANES) + k
+                    st_out[1, b, row:row + 1] = acc[0:1, k * LANES:(k + 1) * LANES]
+                    st_out[1, b, row + 4:row + 5] = top[:, k * LANES:(k + 1) * LANES]
             else:
                 v_acc[b, :, part] = acc
                 v_top[b, :, part] = jnp.broadcast_to(top, (8, BLK))
@@ -243,7 +244,9 @@
         if last:
             t = jnp.where(top_lane, top, acc).T
             num_out[0, a] = t[HEAD:].astype(BF16)
-            st_out[0, a] = t[:8]
+            for k in range(CHUNK // LANES):
+                st_out[0, a, k:k + 1] = t[0:1, k * LANES:(k + 1) * LANES]
+                st_out[0, a, k + 4:k + 5] = t[1:2, k * LANES:(k + 1) * LANES]
             if a:
                 publish(0, a)
         else:
@@ -273,16 +276,16 @@
             following = None
             if n + 1 < len(tiles):
                 following = scores(*tiles[n + 1], places[n + 1])
+            if a or not b:
+                weigh_sensor(a, b, places[n], tops[1], s_count[a] == 0, s_count[a] == NX - 1)
+                s_count[a] += 1
+            else:
+                later.append((weigh_sensor, a, b, places[n], tops[1]))
             if b or not a:
                 weigh_video(a, b, places[n], tops[0], v_count[b] == 0, v_count[b] == NX - 1)
                 v_count[b] += 1
             else:
                 later.append((weigh_video, a, b, places[n], tops[0]))
-            if a or not b:
-                weigh_sensor(a, b, places[n], tops[1], s_count[a] == 0, s_count[a] == NX - 1)
-                s_count[a] += 1
-            else:
-                later.append((weigh_sensor, a, b, places[n], tops[1]))
             tops = following
     for part, a, b, place, top in later:
         part(a, b, place, top, False, a + b == NX - 1)
@@ -301,15 +304,16 @@
             ).wait()
         nums = [num_out[side, 0]] + [num_in[side, o] for o in (1, 2, 3)]
         stats = [st_out[side, 0]] + [st_in[side, o] for o in (1, 2, 3)]
-        highs = [s[1:2] for s in stats]
+        sums = [jnp.concatenate([s[k:k + 1] for k in range(4)], axis=1) for s in stats]
+        highs = [jnp.concatenate([s[k:k + 1] for k in range(4, 8)], axis=1) for s in stats]
         top = jnp.maximum(jnp.maximum(highs[0], highs[1]), jnp.maximum(highs[2], highs[3]))
         total = jnp.zeros((1, CHUNK), F32)
         mixed = jnp.zeros((HEAD, CHUNK), F32)
         for o in range(NX):
             fade = jnp.exp2((highs[o] - top) * C2)
-            total = total + stats[o][0:1] * fade
+            total = total + sums[o] * fade
             mixed = mixed + nums[o].astype(F32) * fade
-        attn = mixed / total
+        attn = mixed * (1.0 / total)
         pair = jnp.concatenate([attn, pltpu.roll(attn, CHUNK - ROWS // 2, 1)], axis=0)
         a_out[side] = pair.T.astype(BF16).reshape(NP, ROWS, LANES)[:, :ROWS // 2]
 
@@ -378,9 +382,9 @@
             pltpu.VMEM((2, NX, NP, ROWS, LANES), BF16),
             pltpu.VMEM((NX, AUG, CHUNK), BF16),
             pltpu.VMEM((2, NX, HEAD, CHUNK), BF16),
-            pltpu.VMEM((2, NX, 8, CHUNK), F32),
+            pltpu.VMEM((2, NX, 8, LANES), F32),
             pltpu.VMEM((2, NX, HEAD, CHUNK), BF16),
-            pltpu.VMEM((2, NX, 8, CHUNK), F32),
+            pltpu.VMEM((2, NX, 8, LANES), F32),
             pltpu.VMEM((2, NP, ROWS // 2, LANES), BF16),
             pltpu.VMEM((2, NP, ROWS // 2, LANES), BF16),
             pltpu.VMEM((NX, CHUNK, LANES), BF16),

time: 47.9 us -> 47.2 us (0.985)
  Pallas kernels: 45.4 us -> 44.7 us
    pallas_call x1, Pallas kernels: 45.4 us -> 44.7 us  [local(): pl.pallas_call(kernel, out_shape=jax.ShapeDtypeStruct((2 * ROWS, D), F32)...]
where the time goes in v3:
time: 47.2 us; the launch traced here: 47.1 us
  Pallas kernels  44.7 us (95%)
  other arithmetic  1.65 us (3%)
  between operations  0.67 us (1%)
    pallas_call x1, Pallas kernels, local(): pl.pallas_call(kernel, out_shape=jax.ShapeDtypeStruct((2 * ROWS, D), F32)...  44.7 us
    convert_element_type x1, other arithmetic, local(): (video.astype(F32) + update[ROWS:]).astype(BF16)  1.65 us

profile of v3, /device:TPU:1, one launch (start us, length us, event | category | flops | bytes accessed | tf_op | source)
XLA Modules:
  0.0 47.1 jit_solution(13445567734409795705)
XLA Ops:
  0.6 0.0 copy-start
  0.6 0.0 copy-start.1
  0.7 44.7 %shard_map.113 = f32[64,1024]{1,0:T(8,128)} custom-call(bf16[32,1024]{1,0:T(8,128)(2,1)} %sensor.1, bf16[32,1024]{1,0:T(8,128)(2,1)} %video.1, bf16[1024,1024]{1,0:T(8,128)(2,1)} %w_sr.1, bf16[1024,1024]{1,0:T(8,128)(2,1)} %w_vr.1, bf16[1024,1024]{1,0:T(8,128)(2,1)} %w_su.1, bf16[1024,1024]{1,0:T(8,128)(2,1)} %w_vu.1, bf16[1024,1024]{1,0:T(8,128)(2,1)} %w_so.1, ...), custom_call_target="tpu_custom_call" | custom-call | tf_op jit(solution)/shard_map/pallas_call | solution.py:374
  45.4 0.0 copy-done
  45.4 0.0 copy-done.1
  45.4 1.6 %add_convert_fusion = (bf16[32,1024]{1,0:T(8,128)(2,1)}, bf16[32,1024]{1,0:T(8,128)(2,1)}) fusion(f32[64,1024]{1,0:T(8,128)} %shard_map.113, bf16[32,1024]{1,0:T(8,128)(2,1)S(1)} %copy-done.1, bf16[32,1024]{1,0:T(8,128)(2,1)S(1)} %copy-done), kind=kLoop, calls=%fused_computation | loop fusion | flops 196608 | bytes 524288 | tf_op jit(solution)/shard_map/convert_element_type | solution.py:420
Async XLA Ops:
  0.6 44.8 %copy-start = (bf16[32,1024]{1,0:T(8,128)(2,1)S(1)}, bf16[32,1024]{1,0:T(8,128)(2,1)}, u32[]{:S(2)}) copy-start(bf16[32,1024]{1,0:T(8,128)(2,1)} %sensor.1) | copy-start | bytes 196612
  0.6 44.8 %copy-start.1 = (bf16[32,1024]{1,0:T(8,128)(2,1)S(1)}, bf16[32,1024]{1,0:T(8,128)(2,1)}, u32[]{:S(2)}) copy-start(bf16[32,1024]{1,0:T(8,128)(2,1)} %video.1) | copy-start | bytes 196612

commit v4 on v3

--- a/solution.py
+++ b/solution.py
@@ -315,27 +315,22 @@
             mixed = mixed + nums[o].astype(F32) * fade
         attn = mixed * (1.0 / total)
         pair = jnp.concatenate([attn, pltpu.roll(attn, CHUNK - ROWS // 2, 1)], axis=0)
-        a_out[side] = pair.T.astype(BF16).reshape(NP, ROWS, LANES)[:, :ROWS // 2]
-
-        def send_back(d, _):
-            s = (core + NP - d) % NP
-            q = (z + shift_z(s // 2) + HALF) % HALF * 2 + s % 2
-            pltpu.make_async_remote_copy(
-                src_ref=a_out.at[side, s], dst_ref=a_in.at[side, p],
-                send_sem=r_send.at[side, q], recv_sem=r_recv.at[side, p],
-                device_id=zc_peer(q), device_id_type=MESH,
-            ).start()
-            return 0
-
-        lax.fori_loop(1, NP, send_back, 0)
-        a_in[side, p] = a_out[side, core]
-
-    def wait_back(side):
+        a_out[:, side] = pair.T.astype(BF16).reshape(NP, ROWS, LANES)[:, :ROWS // 2]
+
+    def send_back(s):
+        there = (z + shift_z(s // 2) + HALF) % HALF
+        pltpu.make_async_remote_copy(
+            src_ref=a_out.at[s], dst_ref=a_in.at[p],
+            send_sem=r_send.at[there * 2 + s % 2], recv_sem=r_recv.at[p],
+            device_id=(there * 4 + x_lo * 2 + s % 2, quarter), device_id_type=MESH,
+        ).start()
+
+    def wait_back():
         def wait(d, _):
             q = (p + d) % NP
             pltpu.make_async_remote_copy(
-                src_ref=a_out.at[side, 0], dst_ref=a_in.at[side, q],
-                send_sem=r_send.at[side, q], recv_sem=r_recv.at[side, q],
+                src_ref=a_out.at[0], dst_ref=a_in.at[q],
+                send_sem=r_send.at[q], recv_sem=r_recv.at[q],
                 device_id=zc_peer(q), device_id_type=MESH,
             ).wait()
             return 0
@@ -345,11 +340,10 @@
     half_low = low[:ROWS // 2]
 
     def finish(side, gain):
-        wait_back(side)
         parts = []
         for k in range(H // 2):
-            a = a_in[side, 2 * k].astype(F32)
-            b = a_in[side, 2 * k + 1].astype(F32)
+            a = a_in[2 * k, side].astype(F32)
+            b = a_in[2 * k + 1, side].astype(F32)
             upper = jnp.where(half_low, a, pltpu.roll(b, HEAD, 1))
             lower = jnp.where(half_low, pltpu.roll(a, HEAD, 1), b)
             parts.append(jnp.concatenate([upper, lower], axis=0))
@@ -363,6 +357,11 @@
     loads[4].wait()
     loads[5].wait()
     combine(1)
+    for s in range(NP - 1, 1, -1):
+        send_back(s)
+    send_back(1 - core)
+    a_in[p] = a_out[core]
+    wait_back()
     finish(0, s_gain)
     finish(1, v_gain)
 
@@ -385,8 +384,8 @@
             pltpu.VMEM((2, NX, 8, LANES), F32),
             pltpu.VMEM((2, NX, HEAD, CHUNK), BF16),
             pltpu.VMEM((2, NX, 8, LANES), F32),
-            pltpu.VMEM((2, NP, ROWS // 2, LANES), BF16),
-            pltpu.VMEM((2, NP, ROWS // 2, LANES), BF16),
+            pltpu.VMEM((NP, 2, ROWS // 2, LANES), BF16),
+            pltpu.VMEM((NP, 2, ROWS // 2, LANES), BF16),
             pltpu.VMEM((NX, CHUNK, LANES), BF16),
             pltpu.VMEM((NX, CHUNK, LANES), BF16),
             pltpu.VMEM((NX, AUG, CHUNK), F32),
@@ -406,7 +405,7 @@
             dma((2, len(GROUPS), NX)), dma((2, len(GROUPS), NX)),
             dma((2, NX)), dma((2, NX)),
             dma((2, NX)), dma((2, NX)),
-            dma((2, NP)), dma((2, NP)),
+            dma((NP,)), dma((NP,)),
         ],
         compiler_params=pltpu.CompilerParams(
             collective_id=0, has_side_effects=True, vmem_limit_bytes=60 * 1024 * 1024

time: 47.2 us -> 46.7 us (0.989)
  Pallas kernels: 44.7 us -> 44.2 us
    pallas_call x1, Pallas kernels: 44.7 us -> 44.2 us  [local(): pl.pallas_call(kernel, out_shape=jax.ShapeDtypeStruct((2 * ROWS, D), F32)...]
where the time goes in v4:
time: 46.7 us; the launch traced here: 46.6 us
  Pallas kernels  44.2 us (95%)
  other arithmetic  1.65 us (4%)
  between operations  0.67 us (1%)
    pallas_call x1, Pallas kernels, local(): pl.pallas_call(kernel, out_shape=jax.ShapeDtypeStruct((2 * ROWS, D), F32)...  44.2 us
    convert_element_type x1, other arithmetic, local(): (video.astype(F32) + update[ROWS:]).astype(BF16)  1.65 us

profile of v4, /device:TPU:1, one launch (start us, length us, event | category | flops | bytes accessed | tf_op | source)
XLA Modules:
  0.0 46.6 jit_solution(5830170878385365436)
XLA Ops:
  0.6 0.0 copy-start
  0.6 0.0 copy-start.1
  0.7 44.2 %shard_map.113 = f32[64,1024]{1,0:T(8,128)} custom-call(bf16[32,1024]{1,0:T(8,128)(2,1)} %sensor.1, bf16[32,1024]{1,0:T(8,128)(2,1)} %video.1, bf16[1024,1024]{1,0:T(8,128)(2,1)} %w_sr.1, bf16[1024,1024]{1,0:T(8,128)(2,1)} %w_vr.1, bf16[1024,1024]{1,0:T(8,128)(2,1)} %w_su.1, bf16[1024,1024]{1,0:T(8,128)(2,1)} %w_vu.1, bf16[1024,1024]{1,0:T(8,128)(2,1)} %w_so.1, ...), custom_call_target="tpu_custom_call" | custom-call | tf_op jit(solution)/shard_map/pallas_call | solution.py:373
  44.9 0.0 copy-done
  44.9 0.0 copy-done.1
  44.9 1.6 %add_convert_fusion = (bf16[32,1024]{1,0:T(8,128)(2,1)}, bf16[32,1024]{1,0:T(8,128)(2,1)}) fusion(f32[64,1024]{1,0:T(8,128)} %shard_map.113, bf16[32,1024]{1,0:T(8,128)(2,1)S(1)} %copy-done.1, bf16[32,1024]{1,0:T(8,128)(2,1)S(1)} %copy-done), kind=kLoop, calls=%fused_computation | loop fusion | flops 196608 | bytes 524288 | tf_op jit(solution)/shard_map/convert_element_type | solution.py:419
Async XLA Ops:
  0.6 44.3 %copy-start = (bf16[32,1024]{1,0:T(8,128)(2,1)S(1)}, bf16[32,1024]{1,0:T(8,128)(2,1)}, u32[]{:S(2)}) copy-start(bf16[32,1024]{1,0:T(8,128)(2,1)} %sensor.1) | copy-start | bytes 196612
  0.6 44.3 %copy-start.1 = (bf16[32,1024]{1,0:T(8,128)(2,1)S(1)}, bf16[32,1024]{1,0:T(8,128)(2,1)}, u32[]{:S(2)}) copy-start(bf16[32,1024]{1,0:T(8,128)(2,1)} %video.1) | copy-start | bytes 196612
